TPU v7x, 256 devices: a whole 4x4x8 slice. The times are simulated.
256 devices in a mesh: seq: 64 (over x, y, z_lo, core), head: 4 (over z_hi).
Axes of the slice: x: 4, y: 4, z: 8 (z_hi: 4, z_lo: 2; z = z_hi * 2 + z_lo), core: 2. Of those that a mesh axis runs over, the one named last changes fastest.
Arguments:
- queries: bfloat16 [32768, 1408], P('seq', 'head'), may hold values from -8 to 8
- keys: bfloat16 [32768, 1408], P('seq', 'head'), may hold values from -8 to 8
- values: bfloat16 [32768, 1408], P('seq', 'head'), may hold values from -6 to 6
- lengths: int32 [16], replicated, may hold values from 1 to 4096, 32768 in all
- out_weight: bfloat16 [1408, 1408], P('head'), may hold values from -0.15625 to 0.15625
Outputs:
- projected: bfloat16 [32768, 1408], P('seq', 'head')
Inputs may be any that keep to these rules, and one draw needn't show every extreme that they name: The lengths sum to 32768, each is 1 or more, and the largest is exactly 4096.
All inputs are finite; a program needn't handle non-finite values.
Results may differ from a plain program's by a relative error of at most 0.017.
Values may be sent and summed in bfloat16 or wider, within the bound.
A program may use at most 64 MiB of HBM per device.

v0:
```python
import jax
import jax.numpy as jnp
from jax import lax
from jax.sharding import PartitionSpec as P

HEAD_DIM = 88


def passed_along(block, axis, distance):
    devices = range(lax.axis_size(axis))
    route = [((i - distance) % len(devices), i) for i in devices]
    return lax.ppermute(block, axis, route)


def body(queries, keys, values, lengths, out_weight):
    tok_rows = queries.shape[0]
    local_heads = queries.shape[1] // HEAD_DIM
    width = lax.axis_size("seq")
    device = lax.axis_index("seq")
    reach = min(8, width // 4)
    scale = 1.0 / HEAD_DIM**0.5
    ends = jnp.cumsum(lengths)
    offsets = jnp.arange(tok_rows, dtype=jnp.int32)

    def video_of(source):
        positions = source * tok_rows + offsets
        found = jnp.sum((ends[None, :] <= positions[:, None]).astype(jnp.int32), axis=1)
        inside = (source >= 0) & (source < width)
        return jnp.where(inside, found, -1)

    video_q = video_of(device)
    query_heads = queries.reshape(tok_rows, local_heads, HEAD_DIM)

    def attend(state, block, video_k):
        running, total, summed = state
        key_heads = block[0].reshape(tok_rows, local_heads, HEAD_DIM)
        value_heads = block[1].reshape(tok_rows, local_heads, HEAD_DIM)
        scores = (
            jnp.einsum("qhd,khd->hqk", query_heads, key_heads, preferred_element_type=jnp.float32)
            * scale
        )
        kept = (video_q[:, None] == video_k[None, :])[None]
        scores = jnp.where(kept, scores, -1e30)
        newest = jnp.maximum(running, jnp.max(scores, axis=-1))
        factor = jnp.exp(running - newest)
        weights = jnp.where(kept, jnp.exp(scores - newest[:, :, None]), 0.0)
        total = total * factor + jnp.sum(weights, axis=-1)
        summed = summed * factor[:, :, None] + jnp.einsum(
            "hqk,khd->hqd",
            weights.astype(jnp.bfloat16),
            value_heads,
            preferred_element_type=jnp.float32,
        )
        return (newest, total, summed)

    def visit(state, block, source):
        video_k = video_of(source)
        touches = (
            (video_k[tok_rows - 1] >= video_q[0])
            & (video_k[0] <= video_q[tok_rows - 1])
            & (video_k[0] >= 0)
            & (source != device)
        )
        return lax.cond(touches, lambda st: attend(st, block, video_k), lambda st: st, state)

    packed = jnp.stack([keys, values])
    state = (
        jnp.full((local_heads, tok_rows), -1e30, jnp.float32),
        jnp.zeros((local_heads, tok_rows), jnp.float32),
        jnp.zeros((local_heads, tok_rows, HEAD_DIM), jnp.float32),
    )
    state = attend(state, packed, video_q)
    farthest = passed_along(packed, "seq", reach)

    def step_along(step, carry):
        block, inner = carry
        inner = visit(inner, block, device - reach + step)
        block = passed_along(block, "seq", -1)
        return (block, inner)

    block, state = lax.fori_loop(0, 2 * reach, step_along, (farthest, state))
    state = visit(state, block, device + reach)
    running, total, summed = state
    attended = summed / total[:, :, None]
    attended = (
        jnp.transpose(attended, (1, 0, 2))
        .reshape(tok_rows, local_heads * HEAD_DIM)
        .astype(jnp.bfloat16)
    )
    partial_terms = jnp.dot(attended, out_weight, preferred_element_type=jnp.float32)
    return lax.psum_scatter(
        partial_terms.astype(jnp.bfloat16), "head", scatter_dimension=1, tiled=True
    )


def solution(mesh):
    in_specs = (P("seq", "head"), P("seq", "head"), P("seq", "head"), P(), P("head", None))
    out_specs = P("seq", "head")
    return jax.shard_map(body, mesh=mesh, in_specs=in_specs, out_specs=out_specs, check_vma=False)
```

profile of v0, /device:TPU:33, one launch (start us, length us, event | category | flops | bytes accessed | tf_op | source)
XLA Modules:
  0.0 330.6 jit_solution(5821497785546285245)
XLA Ops:
  6.5 1.2 pad_maximum_fusion
  7.8 3.0 collective-permute-start.1
  12.6 2.1 fusion.26
  14.8 1.9 copy-done.2
  16.7 1.0 fusion.28
  21.5 4.4 %fusion.32 = f32[4,512,88]{1,2,0:T(8,128)} fusion(bf16[512,4,88]{0,2,1:T(8,128)(2,1)S(1)} %bitcast.37, f32[4,512,512]{1,2,0:T(8,128)} %copy-done.2, f32[4,512]{1,0:T(4,128)S(1)} %broadcast_maximum_fusion, pred[512,512]{0,1:T(8,128)(4,1)S(1)} %broadcast_compare_fusion.2, f32[4,512]{1,0:T(4,128)S(1)} %get-tuple-element.384), kind=kOutput, calls=%fused_computation.40 | convolution fusion | flops 189972480 | bytes 5554176 | tf_op jit(solution)/shard_map/hqk,khd->hqd/dot_general | solution.py:48
  25.9 2.7 collective-permute-done.1
  28.6 234.0 %while.22 = (s32[]{:T(128)}, bf16[2,512,352]{1,2,0:T(8,128)(2,1)S(1)}, f32[4,512]{1,0:T(4,128)S(1)}, f32[4,512]{1,0:T(4,128)S(1)}, f32[4,512,88]{1,2,0:T(8,128)}...) while((s32[]{:T(128)}, ...), condition=%wide.region_11.12_spmd.clone, body=%wide.region_5.11_spmd.clone.sunk | while | flops 383382016 | bytes 27834912 | solution.py:81
  28.6 0.9 copy.33
  29.4 1.5 collective-permute-start
  35.3 5.9 %collective-permute-done = bf16[2,512,352]{1,2,0:T(8,128)(2,1)S(1)} collective-permute-done((bf16[2,512,352]{1,2,0:T(8,128)(2,1)}, bf16[2,512,352]{1,2,0:T(8,128)(2,1)S(1)}, u32[]{:S(2)}, u32[]{:S(2)}) %collective-permute-start) | collective-permute-done | bytes 720928 | tf_op jit(solution)/shard_map/while/body/eval_jaxpr/ppermute | solution.py:12
  46.5 7.4 %collective-permute-done = bf16[2,512,352]{1,2,0:T(8,128)(2,1)S(1)} collective-permute-done((bf16[2,512,352]{1,2,0:T(8,128)(2,1)}, bf16[2,512,352]{1,2,0:T(8,128)(2,1)S(1)}, u32[]{:S(2)}, u32[]{:S(2)}) %collective-permute-start) | collective-permute-done | bytes 720928 | tf_op jit(solution)/shard_map/while/body/eval_jaxpr/ppermute | solution.py:12
  59.2 7.4 %collective-permute-done = bf16[2,512,352]{1,2,0:T(8,128)(2,1)S(1)} collective-permute-done((bf16[2,512,352]{1,2,0:T(8,128)(2,1)}, bf16[2,512,352]{1,2,0:T(8,128)(2,1)S(1)}, u32[]{:S(2)}, u32[]{:S(2)}) %collective-permute-start) | collective-permute-done | bytes 720928 | tf_op jit(solution)/shard_map/while/body/eval_jaxpr/ppermute | solution.py:12
  71.9 7.4 %collective-permute-done = bf16[2,512,352]{1,2,0:T(8,128)(2,1)S(1)} collective-permute-done((bf16[2,512,352]{1,2,0:T(8,128)(2,1)}, bf16[2,512,352]{1,2,0:T(8,128)(2,1)S(1)}, u32[]{:S(2)}, u32[]{:S(2)}) %collective-permute-start) | collective-permute-done | bytes 720928 | tf_op jit(solution)/shard_map/while/body/eval_jaxpr/ppermute | solution.py:12
  84.5 7.4 %collective-permute-done = bf16[2,512,352]{1,2,0:T(8,128)(2,1)S(1)} collective-permute-done((bf16[2,512,352]{1,2,0:T(8,128)(2,1)}, bf16[2,512,352]{1,2,0:T(8,128)(2,1)S(1)}, u32[]{:S(2)}, u32[]{:S(2)}) %collective-permute-start) | collective-permute-done | bytes 720928 | tf_op jit(solution)/shard_map/while/body/eval_jaxpr/ppermute | solution.py:12
  97.2 5.8 %conditional.5 = ((f32[4,512]{1,0:T(4,128)S(1)}, f32[4,512]{1,0:T(4,128)S(1)}, f32[4,512,88]{1,2,0:T(8,128)})) conditional(s32[]{:T(128)} %convert_element_type.78, (f32[4,512]{1,0:T(4,128)S(1)}, f32[4,512]{1,0:T(4,128)S(1)}, f32[4,512,88]{1,2,0:T(8,128)}) %tuple.76, (s32[512]{0:T(512)S(1)}, s32[512]{0:T(512)S(1)}, bf16[2,512,352]{1,2,0:T(8,128)(2,1)}, ...), branch_computations={%region_7.7_spmd, %region_8.10_spmd} | conditional | flops 383356928 | bytes 23498840 | solution.py:64
  97.4 1.1 fusion.39
  98.6 1.0 fusion.2
  99.6 1.0 fusion.4
  100.7 1.4 fusion.8
  103.0 1.7 collective-permute-done
  105.5 1.9 collective-permute-start
  111.8 5.8 %conditional.5 = ((f32[4,512]{1,0:T(4,128)S(1)}, f32[4,512]{1,0:T(4,128)S(1)}, f32[4,512,88]{1,2,0:T(8,128)})) conditional(s32[]{:T(128)} %convert_element_type.78, (f32[4,512]{1,0:T(4,128)S(1)}, f32[4,512]{1,0:T(4,128)S(1)}, f32[4,512,88]{1,2,0:T(8,128)}) %tuple.76, (s32[512]{0:T(512)S(1)}, s32[512]{0:T(512)S(1)}, bf16[2,512,352]{1,2,0:T(8,128)(2,1)}, ...), branch_computations={%region_7.7_spmd, %region_8.10_spmd} | conditional | flops 383356928 | bytes 23498840 | solution.py:64
  112.0 1.1 fusion.39
  113.2 1.0 fusion.2
  114.2 1.0 fusion.4
  115.2 1.4 fusion.8
  117.5 0.9 copy.33
  118.4 6.0 %collective-permute-start = (bf16[2,512,352]{1,2,0:T(8,128)(2,1)}, bf16[2,512,352]{1,2,0:T(8,128)(2,1)S(1)}, u32[]{:S(2)}, u32[]{:S(2)}) collective-permute-start(bf16[2,512,352]{1,2,0:T(8,128)(2,1)} %copy.33), channel_id=1, source_target_pairs={{4,0},{8,4},{12,8},{16,12},{20,16},{24,20},{28,24},{32,28},{36,32}... | collective-permute-start | bytes 2162696 | tf_op jit(solution)/shard_map/while/body/eval_jaxpr/ppermute | solution.py:12
  128.8 5.8 %conditional.5 = ((f32[4,512]{1,0:T(4,128)S(1)}, f32[4,512]{1,0:T(4,128)S(1)}, f32[4,512,88]{1,2,0:T(8,128)})) conditional(s32[]{:T(128)} %convert_element_type.78, (f32[4,512]{1,0:T(4,128)S(1)}, f32[4,512]{1,0:T(4,128)S(1)}, f32[4,512,88]{1,2,0:T(8,128)}) %tuple.76, (s32[512]{0:T(512)S(1)}, s32[512]{0:T(512)S(1)}, bf16[2,512,352]{1,2,0:T(8,128)(2,1)}, ...), branch_computations={%region_7.7_spmd, %region_8.10_spmd} | conditional | flops 383356928 | bytes 23498840 | solution.py:64
  129.0 1.1 fusion.39
  130.2 1.0 fusion.2
  131.2 1.0 fusion.4
  132.3 1.4 fusion.8
  135.4 5.0 %collective-permute-start = (bf16[2,512,352]{1,2,0:T(8,128)(2,1)}, bf16[2,512,352]{1,2,0:T(8,128)(2,1)S(1)}, u32[]{:S(2)}, u32[]{:S(2)}) collective-permute-start(bf16[2,512,352]{1,2,0:T(8,128)(2,1)} %copy.33), channel_id=1, source_target_pairs={{4,0},{8,4},{12,8},{16,12},{20,16},{24,20},{28,24},{32,28},{36,32}... | collective-permute-start | bytes 2162696 | tf_op jit(solution)/shard_map/while/body/eval_jaxpr/ppermute | solution.py:12
  144.8 2.4 collective-permute-done
  148.1 13.0 %collective-permute-start = (bf16[2,512,352]{1,2,0:T(8,128)(2,1)}, bf16[2,512,352]{1,2,0:T(8,128)(2,1)S(1)}, u32[]{:S(2)}, u32[]{:S(2)}) collective-permute-start(bf16[2,512,352]{1,2,0:T(8,128)(2,1)} %copy.33), channel_id=1, source_target_pairs={{4,0},{8,4},{12,8},{16,12},{20,16},{24,20},{28,24},{32,28},{36,32}... | collective-permute-start | bytes 2162696 | tf_op jit(solution)/shard_map/while/body/eval_jaxpr/ppermute | solution.py:12
  165.5 5.8 %conditional.5 = ((f32[4,512]{1,0:T(4,128)S(1)}, f32[4,512]{1,0:T(4,128)S(1)}, f32[4,512,88]{1,2,0:T(8,128)})) conditional(s32[]{:T(128)} %convert_element_type.78, (f32[4,512]{1,0:T(4,128)S(1)}, f32[4,512]{1,0:T(4,128)S(1)}, f32[4,512,88]{1,2,0:T(8,128)}) %tuple.76, (s32[512]{0:T(512)S(1)}, s32[512]{0:T(512)S(1)}, bf16[2,512,352]{1,2,0:T(8,128)(2,1)}, ...), branch_computations={%region_7.7_spmd, %region_8.10_spmd} | conditional | flops 383356928 | bytes 23498840 | solution.py:64
  165.7 1.1 fusion.39
  166.9 1.0 fusion.2
  167.9 1.0 fusion.4
  169.0 1.4 fusion.8
  172.1 1.8 collective-permute-start
  178.3 5.8 %conditional.5 = ((f32[4,512]{1,0:T(4,128)S(1)}, f32[4,512]{1,0:T(4,128)S(1)}, f32[4,512,88]{1,2,0:T(8,128)})) conditional(s32[]{:T(128)} %convert_element_type.78, (f32[4,512]{1,0:T(4,128)S(1)}, f32[4,512]{1,0:T(4,128)S(1)}, f32[4,512,88]{1,2,0:T(8,128)}) %tuple.76, (s32[512]{0:T(512)S(1)}, s32[512]{0:T(512)S(1)}, bf16[2,512,352]{1,2,0:T(8,128)(2,1)}, ...), branch_computations={%region_7.7_spmd, %region_8.10_spmd} | conditional | flops 383356928 | bytes 23498840 | solution.py:64
  178.6 1.1 fusion.39
  179.7 1.0 fusion.2
  180.7 1.0 fusion.4
  181.8 1.4 fusion.8
  185.0 9.2 %collective-permute-start = (bf16[2,512,352]{1,2,0:T(8,128)(2,1)}, bf16[2,512,352]{1,2,0:T(8,128)(2,1)S(1)}, u32[]{:S(2)}, u32[]{:S(2)}) collective-permute-start(bf16[2,512,352]{1,2,0:T(8,128)(2,1)} %copy.33), channel_id=1, source_target_pairs={{4,0},{8,4},{12,8},{16,12},{20,16},{24,20},{28,24},{32,28},{36,32}... | collective-permute-start | bytes 2162696 | tf_op jit(solution)/shard_map/while/body/eval_jaxpr/ppermute | solution.py:12
  198.5 5.8 %conditional.5 = ((f32[4,512]{1,0:T(4,128)S(1)}, f32[4,512]{1,0:T(4,128)S(1)}, f32[4,512,88]{1,2,0:T(8,128)})) conditional(s32[]{:T(128)} %convert_element_type.78, (f32[4,512]{1,0:T(4,128)S(1)}, f32[4,512]{1,0:T(4,128)S(1)}, f32[4,512,88]{1,2,0:T(8,128)}) %tuple.76, (s32[512]{0:T(512)S(1)}, s32[512]{0:T(512)S(1)}, bf16[2,512,352]{1,2,0:T(8,128)(2,1)}, ...), branch_computations={%region_7.7_spmd, %region_8.10_spmd} | conditional | flops 383356928 | bytes 23498840 | solution.py:64
  198.8 1.1 fusion.39
  199.9 1.0 fusion.2
  200.9 1.0 fusion.4
  202.0 1.4 fusion.8
  205.2 6.0 %collective-permute-start = (bf16[2,512,352]{1,2,0:T(8,128)(2,1)}, bf16[2,512,352]{1,2,0:T(8,128)(2,1)S(1)}, u32[]{:S(2)}, u32[]{:S(2)}) collective-permute-start(bf16[2,512,352]{1,2,0:T(8,128)(2,1)} %copy.33), channel_id=1, source_target_pairs={{4,0},{8,4},{12,8},{16,12},{20,16},{24,20},{28,24},{32,28},{36,32}... | collective-permute-start | bytes 2162696 | tf_op jit(solution)/shard_map/while/body/eval_jaxpr/ppermute | solution.py:12
  215.6 1.4 collective-permute-done
  217.8 9.3 %collective-permute-start = (bf16[2,512,352]{1,2,0:T(8,128)(2,1)}, bf16[2,512,352]{1,2,0:T(8,128)(2,1)S(1)}, u32[]{:S(2)}, u32[]{:S(2)}) collective-permute-start(bf16[2,512,352]{1,2,0:T(8,128)(2,1)} %copy.33), channel_id=1, source_target_pairs={{4,0},{8,4},{12,8},{16,12},{20,16},{24,20},{28,24},{32,28},{36,32}... | collective-permute-start | bytes 2162696 | tf_op jit(solution)/shard_map/while/body/eval_jaxpr/ppermute | solution.py:12
  231.6 0.9 copy.33
  232.5 9.7 %collective-permute-start = (bf16[2,512,352]{1,2,0:T(8,128)(2,1)}, bf16[2,512,352]{1,2,0:T(8,128)(2,1)S(1)}, u32[]{:S(2)}, u32[]{:S(2)}) collective-permute-start(bf16[2,512,352]{1,2,0:T(8,128)(2,1)} %copy.33), channel_id=1, source_target_pairs={{4,0},{8,4},{12,8},{16,12},{20,16},{24,20},{28,24},{32,28},{36,32}... | collective-permute-start | bytes 2162696 | tf_op jit(solution)/shard_map/while/body/eval_jaxpr/ppermute | solution.py:12
  246.6 0.9 copy.33
  247.4 10.7 %collective-permute-start = (bf16[2,512,352]{1,2,0:T(8,128)(2,1)}, bf16[2,512,352]{1,2,0:T(8,128)(2,1)S(1)}, u32[]{:S(2)}, u32[]{:S(2)}) collective-permute-start(bf16[2,512,352]{1,2,0:T(8,128)(2,1)} %copy.33), channel_id=1, source_target_pairs={{4,0},{8,4},{12,8},{16,12},{20,16},{24,20},{28,24},{32,28},{36,32}... | collective-permute-start | bytes 2162696 | tf_op jit(solution)/shard_map/while/body/eval_jaxpr/ppermute | solution.py:12
  262.8 1.2 divide_convert_fusion
  264.0 2.1 convolution_convert_fusion
  266.1 57.6 %reduce-scatter.2.cloned.1.call-done = bf16[512,352]{0,1:T(8,128)(2,1)} async-done(((bf16[512,1408]{0,1:T(8,128)(2,1)}), bf16[512,352]{0,1:T(8,128)(2,1)}) %reduce-scatter.2.cloned.1.call-update) | async-done | bytes 360464 | tf_op jit(solution)/shard_map/reduce_scatter | solution.py:91
  (185 shorter events, 40.0 us)
Async XLA Ops:
  6.5 257.4 %copy-start = (bf16[352,1408]{1,0:T(8,128)(2,1)S(1)}, bf16[352,1408]{1,0:T(8,128)(2,1)}, u32[]{:S(2)}) copy-start(bf16[352,1408]{1,0:T(8,128)(2,1)} %param.15) | copy-start | bytes 2973700
  6.5 317.2 %reduce-scatter.2.cloned.1.call-start = ((), (), s32[]{:S(2)}) async-start(), calls=%async_computation.1 | async-start | bytes 1802240 | tf_op jit(solution)/shard_map/reduce_scatter | solution.py:91
  7.8 20.8 %collective-permute-start.1 = (bf16[2,512,352]{1,2,0:T(8,128)(2,1)S(1)}, bf16[2,512,352]{1,2,0:T(8,128)(2,1)S(1)}, u32[]{:S(2)}, u32[]{:S(2)}) collective-permute-start(bf16[2,512,352]{1,2,0:T(8,128)(2,1)S(1)} %pad_maximum_fusion), channel_id=1, source_target_pairs={{224,0},{228,4},{232,8},{236,12},{240,16},{244,20},{248,24},{252,2... | collective-permute-start | bytes 2162696 | tf_op jit(solution)/shard_map/ppermute | solution.py:12
  12.6 8.8 %copy-start.7 = (bf16[512,352]{0,1:T(8,128)(2,1)S(1)}, bf16[512,352]{0,1:T(8,128)(2,1)}, u32[]{:S(2)}) copy-start(bf16[512,352]{0,1:T(8,128)(2,1)} %param.13) | copy-start | bytes 1081348
  14.7 1.9 copy-start.2
  21.5 7.1 %copy-start.1 = (bf16[512,352]{0,1:T(8,128)(2,1)S(1)}, bf16[512,352]{0,1:T(8,128)(2,1)}, u32[]{:S(2)}) copy-start(bf16[512,352]{0,1:T(8,128)(2,1)} %param.11) | copy-start | bytes 1081348
  29.4 11.8 %collective-permute-start = (bf16[2,512,352]{1,2,0:T(8,128)(2,1)}, bf16[2,512,352]{1,2,0:T(8,128)(2,1)S(1)}, u32[]{:S(2)}, u32[]{:S(2)}) collective-permute-start(bf16[2,512,352]{1,2,0:T(8,128)(2,1)} %copy.33), channel_id=1, source_target_pairs={{4,0},{8,4},{12,8},{16,12},{20,16},{24,20},{28,24},{32,28},{36,32}... | collective-permute-start | bytes 2162696 | tf_op jit(solution)/shard_map/while/body/eval_jaxpr/ppermute | solution.py:12
  42.1 11.8 %collective-permute-start = (bf16[2,512,352]{1,2,0:T(8,128)(2,1)}, bf16[2,512,352]{1,2,0:T(8,128)(2,1)S(1)}, u32[]{:S(2)}, u32[]{:S(2)}) collective-permute-start(bf16[2,512,352]{1,2,0:T(8,128)(2,1)} %copy.33), channel_id=1, source_target_pairs={{4,0},{8,4},{12,8},{16,12},{20,16},{24,20},{28,24},{32,28},{36,32}... | collective-permute-start | bytes 2162696 | tf_op jit(solution)/shard_map/while/body/eval_jaxpr/ppermute | solution.py:12
  54.8 11.8 %collective-permute-start = (bf16[2,512,352]{1,2,0:T(8,128)(2,1)}, bf16[2,512,352]{1,2,0:T(8,128)(2,1)S(1)}, u32[]{:S(2)}, u32[]{:S(2)}) collective-permute-start(bf16[2,512,352]{1,2,0:T(8,128)(2,1)} %copy.33), channel_id=1, source_target_pairs={{4,0},{8,4},{12,8},{16,12},{20,16},{24,20},{28,24},{32,28},{36,32}... | collective-permute-start | bytes 2162696 | tf_op jit(solution)/shard_map/while/body/eval_jaxpr/ppermute | solution.py:12
  67.5 11.8 %collective-permute-start = (bf16[2,512,352]{1,2,0:T(8,128)(2,1)}, bf16[2,512,352]{1,2,0:T(8,128)(2,1)S(1)}, u32[]{:S(2)}, u32[]{:S(2)}) collective-permute-start(bf16[2,512,352]{1,2,0:T(8,128)(2,1)} %copy.33), channel_id=1, source_target_pairs={{4,0},{8,4},{12,8},{16,12},{20,16},{24,20},{28,24},{32,28},{36,32}... | collective-permute-start | bytes 2162696 | tf_op jit(solution)/shard_map/while/body/eval_jaxpr/ppermute | solution.py:12
  80.1 11.8 %collective-permute-start = (bf16[2,512,352]{1,2,0:T(8,128)(2,1)}, bf16[2,512,352]{1,2,0:T(8,128)(2,1)S(1)}, u32[]{:S(2)}, u32[]{:S(2)}) collective-permute-start(bf16[2,512,352]{1,2,0:T(8,128)(2,1)} %copy.33), channel_id=1, source_target_pairs={{4,0},{8,4},{12,8},{16,12},{20,16},{24,20},{28,24},{32,28},{36,32}... | collective-permute-start | bytes 2162696 | tf_op jit(solution)/shard_map/while/body/eval_jaxpr/ppermute | solution.py:12
  92.8 11.8 %collective-permute-start = (bf16[2,512,352]{1,2,0:T(8,128)(2,1)}, bf16[2,512,352]{1,2,0:T(8,128)(2,1)S(1)}, u32[]{:S(2)}, u32[]{:S(2)}) collective-permute-start(bf16[2,512,352]{1,2,0:T(8,128)(2,1)} %copy.33), channel_id=1, source_target_pairs={{4,0},{8,4},{12,8},{16,12},{20,16},{24,20},{28,24},{32,28},{36,32}... | collective-permute-start | bytes 2162696 | tf_op jit(solution)/shard_map/while/body/eval_jaxpr/ppermute | solution.py:12
  98.6 2.1 copy-start.3
  102.1 0.9 copy-start.4
  105.5 12.1 %collective-permute-start = (bf16[2,512,352]{1,2,0:T(8,128)(2,1)}, bf16[2,512,352]{1,2,0:T(8,128)(2,1)S(1)}, u32[]{:S(2)}, u32[]{:S(2)}) collective-permute-start(bf16[2,512,352]{1,2,0:T(8,128)(2,1)} %copy.33), channel_id=1, source_target_pairs={{4,0},{8,4},{12,8},{16,12},{20,16},{24,20},{28,24},{32,28},{36,32}... | collective-permute-start | bytes 2162696 | tf_op jit(solution)/shard_map/while/body/eval_jaxpr/ppermute | solution.py:12
  113.1 2.1 copy-start.3
  116.7 0.9 copy-start.4
  118.4 16.2 %collective-permute-start = (bf16[2,512,352]{1,2,0:T(8,128)(2,1)}, bf16[2,512,352]{1,2,0:T(8,128)(2,1)S(1)}, u32[]{:S(2)}, u32[]{:S(2)}) collective-permute-start(bf16[2,512,352]{1,2,0:T(8,128)(2,1)} %copy.33), channel_id=1, source_target_pairs={{4,0},{8,4},{12,8},{16,12},{20,16},{24,20},{28,24},{32,28},{36,32}... | collective-permute-start | bytes 2162696 | tf_op jit(solution)/shard_map/while/body/eval_jaxpr/ppermute | solution.py:12
  130.2 2.1 copy-start.3
  133.7 0.9 copy-start.4
  135.4 11.8 %collective-permute-start = (bf16[2,512,352]{1,2,0:T(8,128)(2,1)}, bf16[2,512,352]{1,2,0:T(8,128)(2,1)S(1)}, u32[]{:S(2)}, u32[]{:S(2)}) collective-permute-start(bf16[2,512,352]{1,2,0:T(8,128)(2,1)} %copy.33), channel_id=1, source_target_pairs={{4,0},{8,4},{12,8},{16,12},{20,16},{24,20},{28,24},{32,28},{36,32}... | collective-permute-start | bytes 2162696 | tf_op jit(solution)/shard_map/while/body/eval_jaxpr/ppermute | solution.py:12
  148.1 23.2 %collective-permute-start = (bf16[2,512,352]{1,2,0:T(8,128)(2,1)}, bf16[2,512,352]{1,2,0:T(8,128)(2,1)S(1)}, u32[]{:S(2)}, u32[]{:S(2)}) collective-permute-start(bf16[2,512,352]{1,2,0:T(8,128)(2,1)} %copy.33), channel_id=1, source_target_pairs={{4,0},{8,4},{12,8},{16,12},{20,16},{24,20},{28,24},{32,28},{36,32}... | collective-permute-start | bytes 2162696 | tf_op jit(solution)/shard_map/while/body/eval_jaxpr/ppermute | solution.py:12
  166.9 2.1 copy-start.3
  170.4 0.9 copy-start.4
  172.1 12.0 %collective-permute-start = (bf16[2,512,352]{1,2,0:T(8,128)(2,1)}, bf16[2,512,352]{1,2,0:T(8,128)(2,1)S(1)}, u32[]{:S(2)}, u32[]{:S(2)}) collective-permute-start(bf16[2,512,352]{1,2,0:T(8,128)(2,1)} %copy.33), channel_id=1, source_target_pairs={{4,0},{8,4},{12,8},{16,12},{20,16},{24,20},{28,24},{32,28},{36,32}... | collective-permute-start | bytes 2162696 | tf_op jit(solution)/shard_map/while/body/eval_jaxpr/ppermute | solution.py:12
  179.7 2.1 copy-start.3
  183.2 0.9 copy-start.4
  185.0 19.4 %collective-permute-start = (bf16[2,512,352]{1,2,0:T(8,128)(2,1)}, bf16[2,512,352]{1,2,0:T(8,128)(2,1)S(1)}, u32[]{:S(2)}, u32[]{:S(2)}) collective-permute-start(bf16[2,512,352]{1,2,0:T(8,128)(2,1)} %copy.33), channel_id=1, source_target_pairs={{4,0},{8,4},{12,8},{16,12},{20,16},{24,20},{28,24},{32,28},{36,32}... | collective-permute-start | bytes 2162696 | tf_op jit(solution)/shard_map/while/body/eval_jaxpr/ppermute | solution.py:12
  199.9 2.1 copy-start.3
  203.4 0.9 copy-start.4
  205.2 11.8 %collective-permute-start = (bf16[2,512,352]{1,2,0:T(8,128)(2,1)}, bf16[2,512,352]{1,2,0:T(8,128)(2,1)S(1)}, u32[]{:S(2)}, u32[]{:S(2)}) collective-permute-start(bf16[2,512,352]{1,2,0:T(8,128)(2,1)} %copy.33), channel_id=1, source_target_pairs={{4,0},{8,4},{12,8},{16,12},{20,16},{24,20},{28,24},{32,28},{36,32}... | collective-permute-start | bytes 2162696 | tf_op jit(solution)/shard_map/while/body/eval_jaxpr/ppermute | solution.py:12
  217.8 13.8 %collective-permute-start = (bf16[2,512,352]{1,2,0:T(8,128)(2,1)}, bf16[2,512,352]{1,2,0:T(8,128)(2,1)S(1)}, u32[]{:S(2)}, u32[]{:S(2)}) collective-permute-start(bf16[2,512,352]{1,2,0:T(8,128)(2,1)} %copy.33), channel_id=1, source_target_pairs={{4,0},{8,4},{12,8},{16,12},{20,16},{24,20},{28,24},{32,28},{36,32}... | collective-permute-start | bytes 2162696 | tf_op jit(solution)/shard_map/while/body/eval_jaxpr/ppermute | solution.py:12
  232.5 14.1 %collective-permute-start = (bf16[2,512,352]{1,2,0:T(8,128)(2,1)}, bf16[2,512,352]{1,2,0:T(8,128)(2,1)S(1)}, u32[]{:S(2)}, u32[]{:S(2)}) collective-permute-start(bf16[2,512,352]{1,2,0:T(8,128)(2,1)} %copy.33), channel_id=1, source_target_pairs={{4,0},{8,4},{12,8},{16,12},{20,16},{24,20},{28,24},{32,28},{36,32}... | collective-permute-start | bytes 2162696 | tf_op jit(solution)/shard_map/while/body/eval_jaxpr/ppermute | solution.py:12
  247.4 15.1 %collective-permute-start = (bf16[2,512,352]{1,2,0:T(8,128)(2,1)}, bf16[2,512,352]{1,2,0:T(8,128)(2,1)S(1)}, u32[]{:S(2)}, u32[]{:S(2)}) collective-permute-start(bf16[2,512,352]{1,2,0:T(8,128)(2,1)} %copy.33), channel_id=1, source_target_pairs={{4,0},{8,4},{12,8},{16,12},{20,16},{24,20},{28,24},{32,28},{36,32}... | collective-permute-start | bytes 2162696 | tf_op jit(solution)/shard_map/while/body/eval_jaxpr/ppermute | solution.py:12
Sparse Core Ops, SparseCore 0:
  266.2 57.4 reduce-scatter.1
where the time goes:
time: 336 us; the launch traced here: 331 us
  waiting for transfers between devices  101 us (30%)
  starting transfers between devices  77.1 us (23%)
  loops' own time  50.8 us (15%)
  local copies, waits for them, and re-layouts  48.3 us (14%)
  matrix products  23.1 us (7%)
  between operations  16.5 us (5%)
  other arithmetic  13.3 us (4%)
    ppermute x17, starting transfers between devices, passed_along(): return lax.ppermute(block, axis, route)  77.1 us
    reduce_scatter x1, waiting for transfers between devices, body(): lax.psum_scatter(partial_terms.astype(jnp.bfloat16), 'head', scatter_dime...  57.6 us
    another operation x1, loops' own time, body(): block, state = lax.fori_loop(0, 2 * reach, step_along, (farthest, state))  50 us
    ppermute x17, waiting for transfers between devices, passed_along(): return lax.ppermute(block, axis, route)  43.7 us
    while x16, local copies, waits for them, and re-layouts  13.7 us
    dot_general x7, matrix products, attend(): jnp.einsum('hqk,khd->hqd', weights.astype(jnp.bfloat16), value_heads, pre...  13 us
    slice x17, local copies, waits for them, and re-layouts, visit(): video_k[0] <= video_q[tok_rows - 1]  10.1 us
    slice x17, local copies, waits for them, and re-layouts, visit(): video_q[tok_rows - 1]  9.84 us
  transfers between devices with their start and end apart: 18, of which 10 were waited for; matrix products, arithmetic and copies ran while one was open for 18% of the time, Pallas kernels for 0%

commit v1 on v0

v1 whole, which is shorter than its diff:
```python
import functools

import jax
import jax.numpy as jnp
from jax import lax
from jax.experimental import pallas as pl
from jax.experimental.pallas import tpu as pltpu
from jax.sharding import PartitionSpec as P

HEAD_DIM = 88
PAD = 96
TOK = 512
QUAD = 4
TILE = 256
SLOTS = 20
EXPONENT = 1.4426950408889634 / HEAD_DIM**0.5
CODE = 1536.0
MESH = pl.DeviceIdType.MESH
F32 = jnp.float32
BF16 = jnp.bfloat16

S_KV, S_Q, S_NEAR, S_FAR, S_W, S_OWN, S_PAIR, S_PART, S_END = 0, 3, 6, 14, 22, 26, 32, 40, 42
R_KV, R_Q, R_W, R_OWN, R_PAIR, R_PART, R_END = 0, 20, 24, 28, 36, 44, 46


def video_code(lengths_ref, first_token, rows, offset):
    shape = (rows, TOK)
    pos = first_token + lax.broadcasted_iota(jnp.int32, shape, 1)
    row = lax.broadcasted_iota(jnp.int32, shape, 0) - offset
    video = jnp.zeros(shape, jnp.int32)
    end = 0
    for i in range(16):
        end = end + lengths_ref[i]
        video = video + jnp.where(pos >= end, 1, 0)
    both = row & video
    parity = (both ^ (both >> 1) ^ (both >> 2) ^ (video >> 3)) & 1
    return (1 - 2 * parity).astype(F32)


def kernel(
    lengths_ref, q_ref, k_ref, v_ref, w_ref, out_ref,
    kvs, qs, win, qw, kp, vp, qn, top, acc, wp, wr, ob, ao, ap, part, part_in,
    send, recv,
):
    seq, h = lax.axis_index("seq"), lax.axis_index("head")
    quads = lax.axis_size("seq") // QUAD
    g, j = seq // QUAD, seq % QUAD
    z, c = j // 2, j % 2
    left = ((g + quads - 1) % quads) * QUAD + j
    right = ((g + 1) % quads) * QUAD + j
    p1 = h + 1 - 2 * (h % 2)
    p2 = 3 - h

    def member(o):
        return 2 * ((z + o // 2) % 2) + (c + o % 2) % 2

    def copy(src, dst, s, r, seq_to, head_to):
        return pltpu.make_async_remote_copy(
            src_ref=src, dst_ref=dst, send_sem=send.at[s], recv_sem=recv.at[r],
            device_id=(seq_to, head_to), device_id_type=MESH,
        )

    barrier = pltpu.get_barrier_semaphore()

    def greet(seq_to, head_to):
        pl.semaphore_signal(barrier, inc=1, device_id=(seq_to, head_to), device_id_type=MESH)

    greet(left, h)
    greet(right, h)
    for o in range(QUAD):
        if o > 0:
            greet(g * QUAD + member(o), h)
        greet(g * QUAD + member(o), p1)
        greet(g * QUAD + member(o), p2)
    pl.semaphore_wait(barrier, 13)

    def one_hot(rows, shift):
        r = lax.broadcasted_iota(jnp.int32, (rows, QUAD * HEAD_DIM), 0) - shift
        col = lax.broadcasted_iota(jnp.int32, (rows, QUAD * HEAD_DIM), 1)
        return r, col

    def pick(hot, x):
        return lax.dot_general(hot, x, (((1,), (1,)), ((), ())), preferred_element_type=F32)

    def head_kv(i):
        r, col = one_hot(2 * HEAD_DIM, 0)
        of_k = jnp.where((r < HEAD_DIM) & (col == r + HEAD_DIM * i), 1.0, 0.0).astype(BF16)
        of_v = jnp.where((r >= HEAD_DIM) & (col == r + HEAD_DIM * (i - 1)), 1.0, 0.0).astype(BF16)
        return (pick(of_k, k_ref[...]) + pick(of_v, v_ref[...])).astype(BF16)

    own_code = video_code(lengths_ref, seq * TOK, PAD, HEAD_DIM)
    row96 = lax.broadcasted_iota(jnp.int32, (PAD, TOK), 0)

    def head_q(i):
        r, col = one_hot(PAD, 0)
        of_q = jnp.where((r < HEAD_DIM) & (col == r + HEAD_DIM * i), 1.0, 0.0).astype(BF16)
        return jnp.where(row96 < HEAD_DIM, pick(of_q, q_ref[...]), own_code).astype(BF16)

    def near(blk):
        for to, slot, way in ((right, 4, 0), (left, 12, 1)):
            copy(win.at[8 + blk], win.at[slot + blk], S_NEAR + 2 * blk + way, R_KV + slot + blk, to, h).start()

    def far(blk):
        for to, src, slot, way in ((right, 4, 0, 0), (left, 12, 16, 1)):
            copy(win.at[src + blk], win.at[slot + blk], S_FAR + 2 * blk + way, R_KV + slot + blk, to, h).start()

    win[8 + j] = head_kv(j)
    near(j)
    for o in (2, 3, 1):
        i = member(o)
        kvs[o - 1] = head_kv(i)
        copy(kvs.at[o - 1], win.at[8 + j], S_KV + o - 1, R_KV + 8 + j, g * QUAD + i, h).start()
    for o in (2, 3, 1):
        i = member(o)
        qs[o - 1] = head_q(i)
        copy(qs.at[o - 1], qw.at[j], S_Q + o - 1, R_Q + j, g * QUAD + i, h).start()
    qw[j] = head_q(j)

    r = lax.broadcasted_iota(jnp.int32, (QUAD * PAD, QUAD * HEAD_DIM), 0)
    col = lax.broadcasted_iota(jnp.int32, (QUAD * PAD, QUAD * HEAD_DIM), 1)
    spread = jnp.where((r % PAD >= PAD - HEAD_DIM) & (col == HEAD_DIM * (r // PAD) + r % PAD - (PAD - HEAD_DIM)), 1.0, 0.0)
    rows = jnp.dot(spread.astype(BF16), w_ref[...], preferred_element_type=F32)
    cols = QUAD * HEAD_DIM
    for b in range(4):
        wp[b] = rows[:, cols * b : cols * (b + 1)].astype(BF16)
    for half, pair, beyond in ((0, p1, 3 - p1), (1, p2, p2 + 1 - 2 * (p2 % 2))):
        for n, block in ((0, pair), (1, beyond)):
            copy(wp.at[block], wr.at[half, n], S_W + 2 * half + n, R_W + 2 * half + n, seq, pair).start()

    row16 = lax.broadcasted_iota(jnp.int32, (16, TOK), 0)

    def arrived(slot):
        copy(win.at[slot], win.at[slot], S_KV, R_KV + slot, seq, h).wait_recv()

    def augment(slot):
        blocks = quads * QUAD
        first = ((g * QUAD + slot - 8 + blocks) % blocks) * TOK
        code = (CODE * video_code(lengths_ref, first, 16, 8)).astype(BF16)
        middle = win[slot, 80:96, :]
        kp[slot, 0:80, :] = win[slot, 0:80, :]
        kp[slot, 80:96, :] = jnp.where(row16 < 8, middle, code)
        vp[slot, 0:16, :] = jnp.where(row16 < 8, jnp.ones_like(middle), middle)
        vp[slot, 16:96, :] = win[slot, 96:176, :]

    augment(8 + j)
    for o in range(1, QUAD):
        blk = member(o)
        arrived(8 + blk)
        near(blk)
        augment(8 + blk)
    for o in range(QUAD):
        blk = member(o)
        if o > 0:
            copy(qw.at[blk], qw.at[blk], S_Q, R_Q + blk, seq, h).wait_recv()
        qn[pl.ds(pl.multiple_of(blk * TOK, TOK), TOK), :] = qw[blk].T
    top[...] = jnp.full(top.shape, -1e30, F32)
    acc[...] = jnp.zeros(acc.shape, F32)

    def attend(at, slots):
        q = qn[at, :]
        scores = [jnp.dot(q, kp[s], preferred_element_type=F32) for s in slots]
        before = top[at, :]
        newest = before
        for s in scores:
            newest = jnp.maximum(newest, jnp.max(s, axis=1, keepdims=True))
        total = acc[at, :] * jnp.exp2((before - newest) * EXPONENT)
        for s, slot in zip(scores, slots):
            weights = jnp.exp2((s - newest) * EXPONENT).astype(BF16)
            total = total + lax.dot_general(
                weights, vp[slot], (((1,), (1,)), ((), ())), preferred_element_type=F32
            )
        return newest, total

    def rows_at(t):
        return pl.ds(pl.multiple_of(t * TILE, TILE), TILE)

    def own_step(o, carry):
        blk = member(o)
        for first in (4, 12):
            arrived(first + blk)
        far(blk)
        for first in (4, 12):
            augment(first + blk)

        def tile(n, carry):
            at = rows_at(2 * o + n)
            newest, total = attend(at, [8, 9, 10, 11])
            top[at, :] = newest
            acc[at, :] = total
            return carry

        return lax.fori_loop(0, 2, tile, carry)

    lax.fori_loop(0, QUAD, own_step, 0)

    def near_step(t, carry):
        at = rows_at(t)
        for slots in ([4, 5, 6, 7], [12, 13, 14, 15]):
            newest, total = attend(at, slots)
            top[at, :] = newest
            acc[at, :] = total
        return carry

    lax.fori_loop(0, 2 * QUAD, near_step, 0)

    def far_in(o, carry):
        blk = member(o)
        for first in (0, 16):
            arrived(first + blk)
            augment(first + blk)
        return carry

    lax.fori_loop(0, QUAD, far_in, 0)

    for half, pair in ((0, p1), (1, p2)):

        def far_step(n, carry):
            o = 3 - n
            b = member(o)
            at = rows_at(2 * b + half)
            newest, total = attend(at, [b + i + 12 * ((b + i) // 4) for i in range(5)])
            done = (total / total[:, 0:1]).T.astype(BF16)
            ob[half, b] = done
            to = g * QUAD + b

            @pl.when(o > 0)
            def _():
                copy(ob.at[half, b], ao.at[half, j], S_OWN + 3 * half + o - 1, R_OWN + 4 * half + j, to, h).start()

            copy(ob.at[half, b], ap.at[half, j], S_PAIR + 4 * half + o, R_PAIR + 4 * half + j, to, pair).start()
            return carry

        lax.fori_loop(0, QUAD, far_step, 0)
        ao[half, j] = ob[half, j]

    for n in range(4):
        copy(wr.at[n // 2, n % 2], wr.at[n // 2, n % 2], S_W, R_W + n, seq, h).wait_recv()
    sums = []
    for half, beyond in ((0, p2), (1, p1)):
        for o in range(QUAD):
            blk = member(o)
            if o > 0:
                copy(ao.at[half, blk], ao.at[half, blk], S_OWN, R_OWN + 4 * half + blk, seq, h).wait_recv()
            copy(ap.at[half, blk], ap.at[half, blk], S_PAIR, R_PAIR + 4 * half + blk, seq, h).wait_recv()
        mine = ao[half].reshape(QUAD * PAD, TILE).T
        other = ap[half].reshape(QUAD * PAD, TILE).T
        part[half] = (
            jnp.dot(mine, wp[beyond], preferred_element_type=F32)
            + jnp.dot(other, wr[half, 1], preferred_element_type=F32)
        ).astype(BF16)
        copy(part.at[half], part_in.at[half], S_PART + half, R_PART + half, seq, beyond).start()
        sums.append(
            jnp.dot(mine, wp[h], preferred_element_type=F32)
            + jnp.dot(other, wr[half, 0], preferred_element_type=F32)
        )
    for half in range(2):
        copy(part_in.at[half], part_in.at[half], S_PART, R_PART + half, seq, h).wait_recv()
        out_ref[half * TILE : (half + 1) * TILE, :] = (sums[half] + part_in[half].astype(F32)).astype(BF16)

    for o in range(3):
        copy(kvs.at[0], kvs.at[0], S_KV + o, R_KV, seq, h).wait_send()
        copy(qs.at[0], qs.at[0], S_Q + o, R_Q, seq, h).wait_send()
    for n in range(16):
        copy(win.at[0], win.at[0], S_NEAR + n, R_KV, seq, h).wait_send()
    for n in range(4):
        copy(wp.at[0], wp.at[0], S_W + n, R_W, seq, h).wait_send()
    for n in range(6):
        copy(ob.at[0, 0], ob.at[0, 0], S_OWN + n, R_OWN, seq, h).wait_send()
    for n in range(8):
        copy(ob.at[0, 0], ob.at[0, 0], S_PAIR + n, R_PAIR, seq, h).wait_send()
    for n in range(2):
        copy(part.at[0], part.at[0], S_PART + n, R_PART, seq, h).wait_send()


def body(queries, keys, values, lengths, out_weight):
    cols = QUAD * HEAD_DIM
    vmem = pl.BlockSpec(memory_space=pltpu.VMEM)
    return pl.pallas_call(
        kernel,
        out_shape=jax.ShapeDtypeStruct((TOK, cols), BF16),
        in_specs=[pl.BlockSpec(memory_space=pltpu.SMEM)] + [vmem] * 4,
        out_specs=vmem,
        scratch_shapes=[
            pltpu.VMEM((3, 2 * HEAD_DIM, TOK), BF16),
            pltpu.VMEM((3, PAD, TOK), BF16),
            pltpu.VMEM((SLOTS, 2 * HEAD_DIM, TOK), BF16),
            pltpu.VMEM((QUAD, PAD, TOK), BF16),
            pltpu.VMEM((SLOTS, PAD, TOK), BF16),
            pltpu.VMEM((SLOTS, PAD, TOK), BF16),
            pltpu.VMEM((QUAD * TOK, PAD), BF16),
            pltpu.VMEM((QUAD * TOK, 1), F32),
            pltpu.VMEM((QUAD * TOK, PAD), F32),
            pltpu.VMEM((4, QUAD * PAD, cols), BF16),
            pltpu.VMEM((2, 2, QUAD * PAD, cols), BF16),
            pltpu.VMEM((2, QUAD, PAD, TILE), BF16),
            pltpu.VMEM((2, QUAD, PAD, TILE), BF16),
            pltpu.VMEM((2, QUAD, PAD, TILE), BF16),
            pltpu.VMEM((2, TILE, cols), BF16),
            pltpu.VMEM((2, TILE, cols), BF16),
            pltpu.SemaphoreType.DMA((S_END,)),
            pltpu.SemaphoreType.DMA((R_END,)),
        ],
        compiler_params=pltpu.CompilerParams(
            collective_id=0, has_side_effects=True, vmem_limit_bytes=56 << 20
        ),
    )(lengths, queries, keys, values, out_weight)


def solution(mesh):
    in_specs = (P("seq", "head"), P("seq", "head"), P("seq", "head"), P(), P("head", None))
    out_specs = P("seq", "head")
    return jax.shard_map(body, mesh=mesh, in_specs=in_specs, out_specs=out_specs, check_vma=False)
```

time: 336 us -> 113 us (0.34)
  the two profiles are of different devices: /device:TPU:33 before, /device:TPU:1 now
where the time goes in v1:
time: 113 us; the launch traced here: 112 us
  Pallas kernels  107 us (95%)
  local copies, waits for them, and re-layouts  5.74 us (5%)
    pallas_call x1, Pallas kernels, body(): pl.pallas_call(kernel, out_shape=jax.ShapeDtypeStruct((TOK, cols), BF16),...  107 us
    unnamed x7, local copies, waits for them, and re-layouts  3.84 us

profile of v1, /device:TPU:1, one launch (start us, length us, event | category | flops | bytes accessed | tf_op | source)
XLA Modules:
  0.0 112.4 jit_solution(16641787211948907825)
XLA Ops:
  0.0 0.0 copy-start
  0.0 1.9 %copy.6.q_ref = bf16[512,352]{1,0:T(8,128)(2,1)} copy(bf16[512,352]{0,1:T(8,128)(2,1)} %param.5) | data formatting | bytes 720896 | tf_op args[0]
  2.0 0.0 copy-done
  2.0 0.0 copy-start.1
  2.0 0.9 copy.7.k_ref
  2.9 0.1 copy-done.1
  2.9 0.9 copy.8.v_ref
  3.8 106.7 %shard_map.55 = bf16[512,352]{1,0:T(8,128)(2,1)} custom-call(s32[16]{0:T(128)} %lengths_ref.1, bf16[512,352]{1,0:T(8,128)(2,1)} %copy.6.q_ref, bf16[512,352]{1,0:T(8,128)(2,1)} %copy.7.k_ref, bf16[512,352]{1,0:T(8,128)(2,1)} %copy.8.v_ref, bf16[352,1408]{1,0:T(8,128)(2,1)} %w_ref.1), custom_call_target="tpu_custom_call" | custom-call | tf_op jit(solution)/shard_map/pallas_call | solution.py:278
  110.5 1.9 %copy.9 = bf16[512,352]{0,1:T(8,128)(2,1)} copy(bf16[512,352]{1,0:T(8,128)(2,1)} %shard_map.55) | data formatting | bytes 720896 | tf_op jit(solution)/shard_map/pallas_call | solution.py:278
Async XLA Ops:
  0.0 2.0 %copy-start = (bf16[512,352]{0,1:T(8,128)(2,1)S(1)}, bf16[512,352]{0,1:T(8,128)(2,1)}, u32[]{:S(2)}) copy-start(bf16[512,352]{0,1:T(8,128)(2,1)} %param.6) | copy-start | bytes 1081348
  2.0 1.0 copy-start.1

commit v2 on v1

v2 whole, which is shorter than its diff:
```python
import functools

import jax
import jax.numpy as jnp
from jax import lax
from jax.experimental import pallas as pl
from jax.experimental.pallas import tpu as pltpu
from jax.sharding import PartitionSpec as P

HEAD_DIM = 88
PAD = 96
TOK = 512
QUAD = 4
TILE = 256
SLOTS = 20
EXPONENT = 1.4426950408889634 / HEAD_DIM**0.5
CODE = 1536.0
MESH = pl.DeviceIdType.MESH
F32 = jnp.float32
BF16 = jnp.bfloat16

S_KV, S_Q, S_NEAR, S_FAR, S_W, S_WQ, S_OWN, S_PAIR, S_PART, S_END = 0, 4, 8, 16, 24, 25, 29, 33, 41, 43
R_KV, R_Q, R_W, R_OWN, R_PAIR, R_PART, R_END = 0, 20, 24, 28, 32, 40, 42


def video_code(lengths_ref, first_token, rows, offset):
    shape = (rows, TOK)
    pos = first_token + lax.broadcasted_iota(jnp.int32, shape, 1)
    row = lax.broadcasted_iota(jnp.int32, shape, 0) - offset
    video = jnp.zeros(shape, jnp.int32)
    end = 0
    for i in range(16):
        end = end + lengths_ref[i]
        video = video + jnp.where(pos >= end, 1, 0)
    both = row & video
    parity = (both ^ (both >> 1) ^ (both >> 2) ^ (video >> 3)) & 1
    return (1 - 2 * parity).astype(F32)


def kernel(
    lengths_ref, q_ref, k_ref, v_ref, w_ref, out_ref,
    kvs, qs, win, qw, kp, vp, qn, top, acc, wp, wr, ob, ao, ap, part, part_in,
    send, recv,
):
    seq, h = lax.axis_index("seq"), lax.axis_index("head")
    quads = lax.axis_size("seq") // QUAD
    g, j = seq // QUAD, seq % QUAD
    z, c = j // 2, j % 2
    left = ((g + quads - 1) % quads) * QUAD + j
    right = ((g + 1) % quads) * QUAD + j
    p1 = h + 1 - 2 * (h % 2)
    p2 = 3 - h

    def member(o):
        return 2 * ((z + o // 2) % 2) + (c + o % 2) % 2

    def copy(src, dst, s, r, seq_to, head_to):
        return pltpu.make_async_remote_copy(
            src_ref=src, dst_ref=dst, send_sem=send.at[s], recv_sem=recv.at[r],
            device_id=(seq_to, head_to), device_id_type=MESH,
        )

    barrier = pltpu.get_barrier_semaphore()

    def greet(seq_to, head_to):
        pl.semaphore_signal(barrier, inc=1, device_id=(seq_to, head_to), device_id_type=MESH)

    greet(left, h)
    greet(right, h)
    for o in range(QUAD):
        if o > 0:
            greet(g * QUAD + member(o), h)
        greet(g * QUAD + member(o), p1)
        greet(g * QUAD + member(o), p2)

    for i in range(QUAD):
        rows = slice(HEAD_DIM * i, HEAD_DIM * (i + 1))
        kvs[i] = jnp.concatenate([k_ref[rows, :], v_ref[rows, :]], axis=0)
    own_code = video_code(lengths_ref, seq * TOK, 8, 0).astype(BF16)
    for i in range(QUAD):
        rows = slice(HEAD_DIM * i, HEAD_DIM * (i + 1))
        qs[i] = jnp.concatenate([q_ref[rows, :], own_code], axis=0)
    pl.semaphore_wait(barrier, 13)

    def near(src, blk):
        for to, slot, way in ((right, 4, 0), (left, 12, 1)):
            copy(src, win.at[slot + blk], S_NEAR + 2 * blk + way, R_KV + slot + blk, to, h).start()

    near(kvs.at[j], j)
    for o in (2, 3, 1):
        i = member(o)
        copy(kvs.at[i], win.at[8 + j], S_KV + o, R_KV + 8 + j, g * QUAD + i, h).start()
    for o in (2, 3, 1):
        i = member(o)
        copy(qs.at[i], qw.at[j], S_Q + o, R_Q + j, g * QUAD + i, h).start()
    win[8 + j] = kvs[j]
    qw[j] = qs[j]

    cols = QUAD * HEAD_DIM
    r = lax.broadcasted_iota(jnp.int32, (cols, QUAD * PAD), 0)
    col = lax.broadcasted_iota(jnp.int32, (cols, QUAD * PAD), 1)
    from_row = HEAD_DIM * (col // PAD) + col % PAD - (PAD - HEAD_DIM)
    spread = jnp.where((col % PAD >= PAD - HEAD_DIM) & (r == from_row), 1.0, 0.0).astype(BF16)
    for b in range(4):
        wp[b] = lax.dot_general(
            w_ref[:, cols * b : cols * (b + 1)], spread, (((0,), (0,)), ((), ())), preferred_element_type=F32
        ).astype(BF16)
    pair = jnp.where(j < 2, p1, p2)
    other = jnp.where(j < 2, 3 - p1, p2 + 1 - 2 * (p2 % 2))
    copy(wp.at[jnp.where(j % 2 == 0, pair, other)], wr.at[j], S_W, R_W + j, seq, pair).start()

    row16 = lax.broadcasted_iota(jnp.int32, (16, TOK), 0)

    def arrived(slot):
        copy(win.at[slot], win.at[slot], S_KV, R_KV + slot, seq, h).wait_recv()

    def augment(slot):
        blocks = quads * QUAD
        first = ((g * QUAD + slot - 8 + blocks) % blocks) * TOK
        code = (CODE * video_code(lengths_ref, first, 16, 8)).astype(BF16)
        middle = win[slot, 80:96, :]
        kp[slot, 0:80, :] = win[slot, 0:80, :]
        kp[slot, 80:96, :] = jnp.where(row16 < 8, middle, code)
        vp[slot, 0:16, :] = jnp.where(row16 < 8, jnp.ones_like(middle), middle)
        vp[slot, 16:96, :] = win[slot, 96:176, :]

    augment(8 + j)
    for o in range(1, QUAD):
        blk = member(o)
        arrived(8 + blk)
        near(win.at[8 + blk], blk)
        augment(8 + blk)
    for o in range(QUAD):
        blk = member(o)
        if o > 0:
            copy(qw.at[blk], qw.at[blk], S_Q, R_Q + blk, seq, h).wait_recv()
        qn[pl.ds(pl.multiple_of(blk * TOK, TOK), TOK), :] = qw[blk].T

    def attend(t, slots, opening=False):
        at = slice(t * TILE, (t + 1) * TILE)
        q = qn[at, :]
        scores = [jnp.dot(q, kp[s], preferred_element_type=F32) for s in slots]
        newest = jnp.max(scores[0], axis=1, keepdims=True)
        for s in scores[1:]:
            newest = jnp.maximum(newest, jnp.max(s, axis=1, keepdims=True))
        total = None
        if not opening:
            before = top[at, :]
            newest = jnp.maximum(before, newest)
            total = acc[at, :] * jnp.exp2((before - newest) * EXPONENT)
        for s, slot in zip(scores, slots):
            weights = jnp.exp2((s - newest) * EXPONENT).astype(BF16)
            term = lax.dot_general(weights, vp[slot], (((1,), (1,)), ((), ())), preferred_element_type=F32)
            total = term if total is None else total + term
        top[at, :] = newest
        acc[at, :] = total

    for t in range(2 * QUAD):
        attend(t, [8, 9, 10, 11], opening=True)

    copy(wr.at[j], wr.at[j], S_W, R_W + j, seq, h).wait_recv()
    for o in range(1, QUAD):
        copy(wr.at[j], wr.at[j], S_WQ + o, R_W + j, g * QUAD + member(o), h).start()

    for n in range(QUAD):
        for to, src, slot, blk, way in ((right, 4, 0, 3 - n, 0), (left, 12, 16, n, 1)):
            arrived(src + blk)
            copy(win.at[src + blk], win.at[slot + blk], S_FAR + 2 * blk + way, R_KV + slot + blk, to, h).start()
    for n in range(QUAD):
        augment(4 + n)
        augment(12 + n)
    for t in range(2 * QUAD):
        attend(t, [4, 5, 6, 7, 12, 13, 14, 15])

    def finish(b):
        for half, pair in ((0, p1), (1, p2)):
            at = slice((2 * b + half) * TILE, (2 * b + half + 1) * TILE)
            total = acc[at, :]
            ob[b, :, half * TILE : (half + 1) * TILE] = (total / total[:, 0:1]).T.astype(BF16)
        to = g * QUAD + b

        @pl.when(j != b)
        def _():
            copy(ob.at[b], ao.at[j], S_OWN + b, R_OWN + j, to, h).start()

        for half, pair in ((0, p1), (1, p2)):
            copy(
                ob.at[b, :, pl.ds(half * TILE, TILE)], ap.at[half, j],
                S_PAIR + 2 * b + half, R_PAIR + 4 * half + j, to, pair,
            ).start()

        @pl.when(j == b)
        def _():
            ao[j] = ob[b]

    def far_round(n, work):
        for slot in (3 - n, 16 + n):
            arrived(slot)
            augment(slot)
        for b, slots in work:
            for half in range(2):
                attend(2 * b + half, slots)

    far_round(0, [(b, [3, 16]) for b in range(4)])
    far_round(1, [(0, [2]), (1, [2, 17]), (2, [2, 17]), (3, [17])])
    far_round(2, [(1, [1]), (2, [18])])
    finish(1)
    finish(2)
    for b, slot in ((0, 1), (3, 18)):
        for half in range(2):
            attend(2 * b + half, [slot])
    far_round(3, [(0, [0]), (3, [19])])
    finish(0)
    finish(3)

    for o in range(1, QUAD):
        blk = member(o)
        copy(wr.at[blk], wr.at[blk], S_W, R_W + blk, seq, h).wait_recv()
    for o in range(1, QUAD):
        blk = member(o)
        copy(ao.at[blk], ao.at[blk], S_OWN, R_OWN + blk, seq, h).wait_recv()
    sums = []
    for half, beyond in ((0, p2), (1, p1)):
        for blk in range(QUAD):
            copy(ap.at[half, blk], ap.at[half, blk], S_PAIR, R_PAIR + 4 * half + blk, seq, h).wait_recv()
        mine = ao[:, :, half * TILE : (half + 1) * TILE].reshape(QUAD * PAD, TILE)
        theirs = ap[half].reshape(QUAD * PAD, TILE)
        part[half] = (
            jnp.dot(wp[beyond], mine, preferred_element_type=F32)
            + jnp.dot(wr[2 * half + 1], theirs, preferred_element_type=F32)
        ).astype(BF16)
        copy(part.at[half], part_in.at[half], S_PART + half, R_PART + half, seq, beyond).start()
        sums.append(
            jnp.dot(wp[h], mine, preferred_element_type=F32)
            + jnp.dot(wr[2 * half], theirs, preferred_element_type=F32)
        )
    for half in range(2):
        copy(part_in.at[half], part_in.at[half], S_PART, R_PART + half, seq, h).wait_recv()
        out_ref[:, half * TILE : (half + 1) * TILE] = (sums[half] + part_in[half].astype(F32)).astype(BF16)

    for o in range(1, QUAD):
        copy(kvs.at[0], kvs.at[0], S_KV + o, R_KV, seq, h).wait_send()
        copy(qs.at[0], qs.at[0], S_Q + o, R_Q, seq, h).wait_send()
        copy(wr.at[0], wr.at[0], S_WQ + o, R_W, seq, h).wait_send()
    for n in range(16):
        copy(win.at[0], win.at[0], S_NEAR + n, R_KV, seq, h).wait_send()
    copy(wp.at[0], wp.at[0], S_W, R_W, seq, h).wait_send()
    for b in range(QUAD):

        @pl.when(j != b)
        def _():
            copy(ob.at[0], ob.at[0], S_OWN + b, R_OWN, seq, h).wait_send()

    for n in range(8):
        copy(ap.at[0, 0], ap.at[0, 0], S_PAIR + n, R_PAIR, seq, h).wait_send()
    for n in range(2):
        copy(part.at[0], part.at[0], S_PART + n, R_PART, seq, h).wait_send()


def body(queries, keys, values, lengths, out_weight):
    cols = QUAD * HEAD_DIM
    vmem = pl.BlockSpec(memory_space=pltpu.VMEM)
    out = pl.pallas_call(
        kernel,
        out_shape=jax.ShapeDtypeStruct((cols, TOK), BF16),
        in_specs=[pl.BlockSpec(memory_space=pltpu.SMEM)] + [vmem] * 4,
        out_specs=vmem,
        scratch_shapes=[
            pltpu.VMEM((QUAD, 2 * HEAD_DIM, TOK), BF16),
            pltpu.VMEM((QUAD, PAD, TOK), BF16),
            pltpu.VMEM((SLOTS, 2 * HEAD_DIM, TOK), BF16),
            pltpu.VMEM((QUAD, PAD, TOK), BF16),
            pltpu.VMEM((SLOTS, PAD, TOK), BF16),
            pltpu.VMEM((SLOTS, PAD, TOK), BF16),
            pltpu.VMEM((QUAD * TOK, PAD), BF16),
            pltpu.VMEM((QUAD * TOK, 1), F32),
            pltpu.VMEM((QUAD * TOK, PAD), F32),
            pltpu.VMEM((4, cols, QUAD * PAD), BF16),
            pltpu.VMEM((4, cols, QUAD * PAD), BF16),
            pltpu.VMEM((QUAD, PAD, TOK), BF16),
            pltpu.VMEM((QUAD, PAD, TOK), BF16),
            pltpu.VMEM((2, QUAD, PAD, TILE), BF16),
            pltpu.VMEM((2, cols, TILE), BF16),
            pltpu.VMEM((2, cols, TILE), BF16),
            pltpu.SemaphoreType.DMA((S_END,)),
            pltpu.SemaphoreType.DMA((R_END,)),
        ],
        compiler_params=pltpu.CompilerParams(
            collective_id=0, has_side_effects=True, vmem_limit_bytes=56 << 20
        ),
    )(lengths, queries.T, keys.T, values.T, out_weight)
    return out.T


def solution(mesh):
    in_specs = (P("seq", "head"), P("seq", "head"), P("seq", "head"), P(), P("head", None))
    out_specs = P("seq", "head")
    return jax.shard_map(body, mesh=mesh, in_specs=in_specs, out_specs=out_specs, check_vma=False)
```

time: 113 us -> 82.5 us (0.73)
  the two profiles are of different devices: /device:TPU:1 before, /device:TPU:33 now
where the time goes in v2:
time: 82.5 us; the launch traced here: 82.3 us
  Pallas kernels  80.6 us (98%)
  local copies, waits for them, and re-layouts  1.74 us (2%)
    pallas_call x1, Pallas kernels, body(): pl.pallas_call(kernel, out_shape=jax.ShapeDtypeStruct((cols, TOK), BF16),...  80.6 us
    unnamed x1, local copies, waits for them, and re-layouts  1.74 us

profile of v2, /device:TPU:33, one launch (start us, length us, event | category | flops | bytes accessed | tf_op | source)
XLA Modules:
  0.0 82.3 jit_solution(11613098254434935105)
XLA Ops:
  0.0 80.6 %shard_map.55 = bf16[352,512]{1,0:T(8,128)(2,1)} custom-call(s32[16]{0:T(128)} %lengths_ref.1, bf16[352,512]{1,0:T(8,128)(2,1)} %bitcast.5, bf16[352,512]{1,0:T(8,128)(2,1)} %bitcast.6, bf16[352,512]{1,0:T(8,128)(2,1)} %bitcast.7, bf16[352,1408]{1,0:T(8,128)(2,1)} %w_ref.1), custom_call_target="tpu_custom_call" | custom-call | tf_op jit(solution)/shard_map/pallas_call | solution.py:263
  80.6 1.7 %copy.7 = bf16[512,352]{0,1:T(8,128)(2,1)} copy(bf16[512,352]{0,1:T(8,128)(2,1)} %bitcast.4) | data formatting | bytes 720896

commit v3 on v2

--- a/solution.py
+++ b/solution.py
@@ -105,9 +105,14 @@
         wp[b] = lax.dot_general(
             w_ref[:, cols * b : cols * (b + 1)], spread, (((0,), (0,)), ((), ())), preferred_element_type=F32
         ).astype(BF16)
-    pair = jnp.where(j < 2, p1, p2)
-    other = jnp.where(j < 2, 3 - p1, p2 + 1 - 2 * (p2 % 2))
-    copy(wp.at[jnp.where(j % 2 == 0, pair, other)], wr.at[j], S_W, R_W + j, seq, pair).start()
+    to_pair = jnp.where(z == 1, (h + 1) % 4, (h + 3) % 4)
+    pair_1 = to_pair + 1 - 2 * (to_pair % 2)
+    beyond = jnp.where(pair_1 == h, 3 - to_pair, pair_1)
+    piece = 2 * (1 - (h + z) % 2) + c
+    copy(
+        wp.at[jnp.where(c == 0, to_pair, beyond)], wr.at[piece], S_W, R_W + piece,
+        g * QUAD + 2 * (1 - z) + c, to_pair,
+    ).start()
 
     row16 = lax.broadcasted_iota(jnp.int32, (16, TOK), 0)
 
@@ -124,20 +129,11 @@
         vp[slot, 0:16, :] = jnp.where(row16 < 8, jnp.ones_like(middle), middle)
         vp[slot, 16:96, :] = win[slot, 96:176, :]
 
-    augment(8 + j)
-    for o in range(1, QUAD):
-        blk = member(o)
-        arrived(8 + blk)
-        near(win.at[8 + blk], blk)
-        augment(8 + blk)
-    for o in range(QUAD):
-        blk = member(o)
-        if o > 0:
-            copy(qw.at[blk], qw.at[blk], S_Q, R_Q + blk, seq, h).wait_recv()
+    def queries_of(blk):
         qn[pl.ds(pl.multiple_of(blk * TOK, TOK), TOK), :] = qw[blk].T
 
     def attend(t, slots, opening=False):
-        at = slice(t * TILE, (t + 1) * TILE)
+        at = pl.ds(t * TILE if isinstance(t, int) else pl.multiple_of(t * TILE, TILE), TILE)
         q = qn[at, :]
         scores = [jnp.dot(q, kp[s], preferred_element_type=F32) for s in slots]
         newest = jnp.max(scores[0], axis=1, keepdims=True)
@@ -155,22 +151,53 @@
         top[at, :] = newest
         acc[at, :] = total
 
-    for t in range(2 * QUAD):
-        attend(t, [8, 9, 10, 11], opening=True)
-
-    copy(wr.at[j], wr.at[j], S_W, R_W + j, seq, h).wait_recv()
-    for o in range(1, QUAD):
-        copy(wr.at[j], wr.at[j], S_WQ + o, R_W + j, g * QUAD + member(o), h).start()
-
+    def attend_block(blk, slots, opening=False):
+        for half in range(2):
+            attend(2 * blk + half, slots, opening)
+
+    here, there = [j, member(1)], [member(2), member(3)]
+
+    augment(8 + j)
+    queries_of(j)
+    arrived(8 + here[1])
+    near(win.at[8 + here[1]], here[1])
+    augment(8 + here[1])
+    copy(qw.at[here[1]], qw.at[here[1]], S_Q, R_Q + here[1], seq, h).wait_recv()
+    queries_of(here[1])
+    for blk in here:
+        attend_block(blk, [8 + i for i in here], opening=True)
+    for blk in there:
+        arrived(8 + blk)
+        near(win.at[8 + blk], blk)
+    for blk in there:
+        augment(8 + blk)
+    for blk in here:
+        for first in (4, 12):
+            arrived(first + blk)
+            augment(first + blk)
+    early = [first + i for first in (4, 12) for i in here]
+    for blk in here:
+        attend_block(blk, [8 + i for i in there] + early)
+    for blk in there:
+        copy(qw.at[blk], qw.at[blk], S_Q, R_Q + blk, seq, h).wait_recv()
+        queries_of(blk)
+    for blk in there:
+        attend_block(blk, [8, 9, 10, 11] + early, opening=True)
+
+    for blk in there:
+        for first in (4, 12):
+            arrived(first + blk)
     for n in range(QUAD):
         for to, src, slot, blk, way in ((right, 4, 0, 3 - n, 0), (left, 12, 16, n, 1)):
-            arrived(src + blk)
             copy(win.at[src + blk], win.at[slot + blk], S_FAR + 2 * blk + way, R_KV + slot + blk, to, h).start()
-    for n in range(QUAD):
-        augment(4 + n)
-        augment(12 + n)
-    for t in range(2 * QUAD):
-        attend(t, [4, 5, 6, 7, 12, 13, 14, 15])
+    copy(wr.at[piece], wr.at[piece], S_W, R_W + piece, seq, h).wait_recv()
+    for o in range(1, QUAD):
+        copy(wr.at[piece], wr.at[piece], S_WQ + o, R_W + piece, g * QUAD + member(o), h).start()
+    for blk in there:
+        for first in (4, 12):
+            augment(first + blk)
+    for blk in range(QUAD):
+        attend_block(blk, [first + i for first in (4, 12) for i in there])
 
     def finish(b):
         for half, pair in ((0, p1), (1, p2)):
@@ -198,8 +225,7 @@
             arrived(slot)
             augment(slot)
         for b, slots in work:
-            for half in range(2):
-                attend(2 * b + half, slots)
+            attend_block(b, slots)
 
     far_round(0, [(b, [3, 16]) for b in range(4)])
     far_round(1, [(0, [2]), (1, [2, 17]), (2, [2, 17]), (3, [17])])
@@ -207,15 +233,15 @@
     finish(1)
     finish(2)
     for b, slot in ((0, 1), (3, 18)):
-        for half in range(2):
-            attend(2 * b + half, [slot])
+        attend_block(b, [slot])
     far_round(3, [(0, [0]), (3, [19])])
     finish(0)
     finish(3)
 
     for o in range(1, QUAD):
-        blk = member(o)
-        copy(wr.at[blk], wr.at[blk], S_W, R_W + blk, seq, h).wait_recv()
+        i = member(o)
+        i = 2 * (1 - (h + i // 2) % 2) + i % 2
+        copy(wr.at[i], wr.at[i], S_W, R_W + i, seq, h).wait_recv()
     for o in range(1, QUAD):
         blk = member(o)
         copy(ao.at[blk], ao.at[blk], S_OWN, R_OWN + blk, seq, h).wait_recv()

time: 82.5 us -> 76.3 us (0.925)
  Pallas kernels: 80.6 us -> 74.4 us
    pallas_call x1, Pallas kernels: 80.6 us -> 74.4 us  [body(): pl.pallas_call(kernel, out_shape=jax.ShapeDtypeStruct((cols, TOK), BF16),...]
where the time goes in v3:
time: 76.3 us; the launch traced here: 76.2 us
  Pallas kernels  74.4 us (98%)
  local copies, waits for them, and re-layouts  1.74 us (2%)
    pallas_call x1, Pallas kernels, body(): pl.pallas_call(kernel, out_shape=jax.ShapeDtypeStruct((cols, TOK), BF16),...  74.4 us
    unnamed x1, local copies, waits for them, and re-layouts  1.74 us

profile of v3, /device:TPU:33, one launch (start us, length us, event | category | flops | bytes accessed | tf_op | source)
XLA Modules:
  0.0 76.2 jit_solution(2750039695471078883)
XLA Ops:
  0.0 74.4 %shard_map.55 = bf16[352,512]{1,0:T(8,128)(2,1)} custom-call(s32[16]{0:T(128)} %lengths_ref.1, bf16[352,512]{1,0:T(8,128)(2,1)} %bitcast.5, bf16[352,512]{1,0:T(8,128)(2,1)} %bitcast.6, bf16[352,512]{1,0:T(8,128)(2,1)} %bitcast.7, bf16[352,1408]{1,0:T(8,128)(2,1)} %w_ref.1), custom_call_target="tpu_custom_call" | custom-call | tf_op jit(solution)/shard_map/pallas_call | solution.py:289
  74.5 1.7 %copy.7 = bf16[512,352]{0,1:T(8,128)(2,1)} copy(bf16[512,352]{0,1:T(8,128)(2,1)} %bitcast.4) | data formatting | bytes 720896

commit v4 on v3

--- a/solution.py
+++ b/solution.py
@@ -86,10 +86,11 @@
         for to, slot, way in ((right, 4, 0), (left, 12, 1)):
             copy(src, win.at[slot + blk], S_NEAR + 2 * blk + way, R_KV + slot + blk, to, h).start()
 
-    near(kvs.at[j], j)
     for o in (2, 3, 1):
         i = member(o)
         copy(kvs.at[i], win.at[8 + j], S_KV + o, R_KV + 8 + j, g * QUAD + i, h).start()
+        if o == 2:
+            near(kvs.at[j], j)
     for o in (2, 3, 1):
         i = member(o)
         copy(qs.at[i], qw.at[j], S_Q + o, R_Q + j, g * QUAD + i, h).start()
@@ -206,15 +207,15 @@
             ob[b, :, half * TILE : (half + 1) * TILE] = (total / total[:, 0:1]).T.astype(BF16)
         to = g * QUAD + b
 
-        @pl.when(j != b)
-        def _():
-            copy(ob.at[b], ao.at[j], S_OWN + b, R_OWN + j, to, h).start()
-
         for half, pair in ((0, p1), (1, p2)):
             copy(
                 ob.at[b, :, pl.ds(half * TILE, TILE)], ap.at[half, j],
                 S_PAIR + 2 * b + half, R_PAIR + 4 * half + j, to, pair,
             ).start()
+
+        @pl.when(j != b)
+        def _():
+            copy(ob.at[b], ao.at[j], S_OWN + b, R_OWN + j, to, h).start()
 
         @pl.when(j == b)
         def _():

time: 76.3 us -> 76 us (level)
  no operation moved by 1% of the time
where the time goes in v4:
time: 76 us; the launch traced here: 75.5 us
  Pallas kernels  73.7 us (97%)
  local copies, waits for them, and re-layouts  1.74 us (2%)
    pallas_call x1, Pallas kernels, body(): pl.pallas_call(kernel, out_shape=jax.ShapeDtypeStruct((cols, TOK), BF16),...  73.7 us
    unnamed x1, local copies, waits for them, and re-layouts  1.74 us

profile of v4, /device:TPU:33, one launch (start us, length us, event | category | flops | bytes accessed | tf_op | source)
XLA Modules:
  0.0 75.5 jit_solution(18102538050649168852)
XLA Ops:
  0.0 73.7 %shard_map.55 = bf16[352,512]{1,0:T(8,128)(2,1)} custom-call(s32[16]{0:T(128)} %lengths_ref.1, bf16[352,512]{1,0:T(8,128)(2,1)} %bitcast.5, bf16[352,512]{1,0:T(8,128)(2,1)} %bitcast.6, bf16[352,512]{1,0:T(8,128)(2,1)} %bitcast.7, bf16[352,1408]{1,0:T(8,128)(2,1)} %w_ref.1), custom_call_target="tpu_custom_call" | custom-call | tf_op jit(solution)/shard_map/pallas_call | solution.py:290
  73.7 1.7 %copy.7 = bf16[512,352]{0,1:T(8,128)(2,1)} copy(bf16[512,352]{0,1:T(8,128)(2,1)} %bitcast.4) | data formatting | bytes 720896

commit v5 on v4

--- a/solution.py
+++ b/solution.py
@@ -110,6 +110,7 @@
     pair_1 = to_pair + 1 - 2 * (to_pair % 2)
     beyond = jnp.where(pair_1 == h, 3 - to_pair, pair_1)
     piece = 2 * (1 - (h + z) % 2) + c
+
     copy(
         wp.at[jnp.where(c == 0, to_pair, beyond)], wr.at[piece], S_W, R_W + piece,
         g * QUAD + 2 * (1 - z) + c, to_pair,
@@ -133,28 +134,39 @@
     def queries_of(blk):
         qn[pl.ds(pl.multiple_of(blk * TOK, TOK), TOK), :] = qw[blk].T
 
-    def attend(t, slots, opening=False):
-        at = pl.ds(t * TILE if isinstance(t, int) else pl.multiple_of(t * TILE, TILE), TILE)
-        q = qn[at, :]
-        scores = [jnp.dot(q, kp[s], preferred_element_type=F32) for s in slots]
-        newest = jnp.max(scores[0], axis=1, keepdims=True)
-        for s in scores[1:]:
-            newest = jnp.maximum(newest, jnp.max(s, axis=1, keepdims=True))
-        total = None
-        if not opening:
-            before = top[at, :]
-            newest = jnp.maximum(before, newest)
-            total = acc[at, :] * jnp.exp2((before - newest) * EXPONENT)
-        for s, slot in zip(scores, slots):
-            weights = jnp.exp2((s - newest) * EXPONENT).astype(BF16)
-            term = lax.dot_general(weights, vp[slot], (((1,), (1,)), ((), ())), preferred_element_type=F32)
-            total = term if total is None else total + term
-        top[at, :] = newest
-        acc[at, :] = total
-
-    def attend_block(blk, slots, opening=False):
-        for half in range(2):
-            attend(2 * blk + half, slots, opening)
+    def attend(work, opening=False):
+        tiles = []
+        for blk, slots in work:
+            for half in range(2):
+                parts = []
+                for slot in slots:
+                    inner = isinstance(blk, int) and isinstance(slot, int)
+                    lo = TILE if inner and half == 1 and slot == blk else 0
+                    hi = TILE if inner and half == 0 and slot == blk + 16 else TOK
+                    parts.append((slot, lo, hi))
+                t = 2 * blk + half
+                at = pl.ds(t * TILE if isinstance(t, int) else pl.multiple_of(t * TILE, TILE), TILE)
+                before = (None, None) if opening else (top[at, :], acc[at, :])
+                tiles.append((at, qn[at, :], *before, parts))
+        results = []
+        for at, q, before, total, parts in tiles:
+            scores = [jnp.dot(q, kp[s, :, lo:hi], preferred_element_type=F32) for s, lo, hi in parts]
+            newest = before
+            for s in scores:
+                most = jnp.max(s, axis=1, keepdims=True)
+                newest = most if newest is None else jnp.maximum(newest, most)
+            if not opening:
+                total = total * jnp.exp2((before - newest) * EXPONENT)
+            for s, (slot, lo, hi) in zip(scores, parts):
+                weights = jnp.exp2((s - newest) * EXPONENT).astype(BF16)
+                term = lax.dot_general(
+                    weights, vp[slot, :, lo:hi], (((1,), (1,)), ((), ())), preferred_element_type=F32
+                )
+                total = term if total is None else total + term
+            results.append((at, newest, total))
+        for at, newest, total in results:
+            top[at, :] = newest
+            acc[at, :] = total
 
     here, there = [j, member(1)], [member(2), member(3)]
 
@@ -165,46 +177,45 @@
     augment(8 + here[1])
     copy(qw.at[here[1]], qw.at[here[1]], S_Q, R_Q + here[1], seq, h).wait_recv()
     queries_of(here[1])
-    for blk in here:
-        attend_block(blk, [8 + i for i in here], opening=True)
+    attend([(blk, [8 + i for i in here]) for blk in here], opening=True)
     for blk in there:
         arrived(8 + blk)
         near(win.at[8 + blk], blk)
     for blk in there:
         augment(8 + blk)
+    attend([(blk, [8 + i for i in there]) for blk in here])
+    for blk in there:
+        copy(qw.at[blk], qw.at[blk], S_Q, R_Q + blk, seq, h).wait_recv()
+        queries_of(blk)
+    attend([(blk, [8, 9, 10, 11]) for blk in there], opening=True)
+    copy(wr.at[piece], wr.at[piece], S_W, R_W + piece, seq, h).wait_recv()
+    for o in range(1, QUAD):
+        copy(wr.at[piece], wr.at[piece], S_WQ + o, R_W + piece, g * QUAD + member(o), h).start()
     for blk in here:
         for first in (4, 12):
             arrived(first + blk)
             augment(first + blk)
     early = [first + i for first in (4, 12) for i in here]
-    for blk in here:
-        attend_block(blk, [8 + i for i in there] + early)
-    for blk in there:
-        copy(qw.at[blk], qw.at[blk], S_Q, R_Q + blk, seq, h).wait_recv()
-        queries_of(blk)
-    for blk in there:
-        attend_block(blk, [8, 9, 10, 11] + early, opening=True)
-
+    attend([(blk, early) for blk in range(3)])
     for blk in there:
         for first in (4, 12):
             arrived(first + blk)
+
     for n in range(QUAD):
         for to, src, slot, blk, way in ((right, 4, 0, 3 - n, 0), (left, 12, 16, n, 1)):
             copy(win.at[src + blk], win.at[slot + blk], S_FAR + 2 * blk + way, R_KV + slot + blk, to, h).start()
-    copy(wr.at[piece], wr.at[piece], S_W, R_W + piece, seq, h).wait_recv()
-    for o in range(1, QUAD):
-        copy(wr.at[piece], wr.at[piece], S_WQ + o, R_W + piece, g * QUAD + member(o), h).start()
+
+    attend([(3, early)])
     for blk in there:
         for first in (4, 12):
             augment(first + blk)
-    for blk in range(QUAD):
-        attend_block(blk, [first + i for first in (4, 12) for i in there])
+    attend([(blk, [first + i for first in (4, 12) for i in there]) for blk in range(QUAD)])
 
     def finish(b):
         for half, pair in ((0, p1), (1, p2)):
             at = slice((2 * b + half) * TILE, (2 * b + half + 1) * TILE)
             total = acc[at, :]
-            ob[b, :, half * TILE : (half + 1) * TILE] = (total / total[:, 0:1]).T.astype(BF16)
+            ob[b, :, half * TILE : (half + 1) * TILE] = (total / total[:, 0:1]).astype(BF16).T
         to = g * QUAD + b
 
         for half, pair in ((0, p1), (1, p2)):
@@ -225,16 +236,14 @@
         for slot in (3 - n, 16 + n):
             arrived(slot)
             augment(slot)
-        for b, slots in work:
-            attend_block(b, slots)
+        attend(work)
 
     far_round(0, [(b, [3, 16]) for b in range(4)])
     far_round(1, [(0, [2]), (1, [2, 17]), (2, [2, 17]), (3, [17])])
     far_round(2, [(1, [1]), (2, [18])])
     finish(1)
     finish(2)
-    for b, slot in ((0, 1), (3, 18)):
-        attend_block(b, [slot])
+    attend([(0, [1]), (3, [18])])
     far_round(3, [(0, [0]), (3, [19])])
     finish(0)
     finish(3)

time: 76 us -> 76 us (level)
  no operation moved by 1% of the time
where the time goes in v5:
time: 76 us; the launch traced here: 75.9 us
  Pallas kernels  74.1 us (97%)
  local copies, waits for them, and re-layouts  1.74 us (2%)
    pallas_call x1, Pallas kernels, body(): pl.pallas_call(kernel, out_shape=jax.ShapeDtypeStruct((cols, TOK), BF16),...  74.1 us
    unnamed x1, local copies, waits for them, and re-layouts  1.74 us

profile of v5, /device:TPU:33, one launch (start us, length us, event | category | flops | bytes accessed | tf_op | source)
XLA Modules:
  0.0 75.9 jit_solution(8000597484309577574)
XLA Ops:
  0.0 74.1 %shard_map.55 = bf16[352,512]{1,0:T(8,128)(2,1)} custom-call(s32[16]{0:T(128)} %lengths_ref.1, bf16[352,512]{1,0:T(8,128)(2,1)} %bitcast.5, bf16[352,512]{1,0:T(8,128)(2,1)} %bitcast.6, bf16[352,512]{1,0:T(8,128)(2,1)} %bitcast.7, bf16[352,1408]{1,0:T(8,128)(2,1)} %w_ref.1), custom_call_target="tpu_custom_call" | custom-call | tf_op jit(solution)/shard_map/pallas_call | solution.py:299
  74.1 1.7 %copy.7 = bf16[512,352]{0,1:T(8,128)(2,1)} copy(bf16[512,352]{0,1:T(8,128)(2,1)} %bitcast.4) | data formatting | bytes 720896
